TPU v7x, 32 devices: a whole 2x2x4 slice. The times are simulated.
32 devices in a mesh: dp: 2 (over y), mp: 16 (over z, x, core).
Axes of the slice: x: 2, y: 2, z: 4, core: 2. Of those that a mesh axis runs over, the one named last changes fastest.
Arguments:
- attn_out: bfloat16 [1024, 8192], P('dp', 'mp'), may hold values from -6 to 6
- grad_out: bfloat16 [1024, 8192], P(('dp', 'mp')), may hold values from -0.26367188 to 0.26367188
- proj_weight: bfloat16 [8192, 8192], P('mp'), may hold values from -1.5 to 1.5
- error_buf: bfloat16 [2, 8192, 8192], P('dp', 'mp'), may hold values from -6 to 6
- q_start: float32 [8192, 32], P('mp'), may hold values from -6 to 6
Outputs:
- new_error: bfloat16 [2, 8192, 8192], P('dp', 'mp')
- q_factor: float32 [8192, 32], P('mp')
- d_attn: bfloat16 [1024, 8192], P('dp', 'mp')
All inputs are finite; a program needn't handle non-finite values.
Results may differ from a plain program's by a relative error of at most 0.012.
Values may be sent and summed in bfloat16 or wider, within the bound.
A program may use at most 128 MiB of HBM per device.

v0:
```python
import jax
import jax.numpy as jnp
from jax import lax
from jax.sharding import PartitionSpec as P


def full_gradient(attn_out, grad_out, proj_weight):
    piece = lax.all_gather(grad_out, "mp", axis=0, tiled=True)
    total = lax.dot_general(
        attn_out, piece, (((0,), (0,)), ((), ())), preferred_element_type=jnp.float32
    )
    rows = lax.dot_general(
        piece, proj_weight, (((1,), (1,)), ((), ())), preferred_element_type=jnp.float32
    )
    cotangent = rows
    total, cotangent = (total, cotangent)
    return (total, cotangent.astype(jnp.bfloat16))


def on_device(attn_out, grad_out, proj_weight, error_buf, q_start):
    hp = lax.Precision.HIGHEST
    replicas = lax.axis_size("dp")
    own_count = q_start.shape[0]
    q_full = lax.all_gather(q_start, "mp", axis=0, tiled=True)
    error_local = error_buf[0].astype(jnp.float32)
    gradient, d_attn = full_gradient(attn_out, grad_out, proj_weight)
    moment = gradient + error_local
    p_local = jnp.dot(moment, q_full, precision=hp)
    p_mean = lax.psum(p_local.astype(jnp.bfloat16), "dp").astype(jnp.float32) / replicas
    gram_sum = lax.psum(jnp.dot(p_mean.T, p_mean, precision=hp), "mp")
    lower_factor = jnp.linalg.cholesky(gram_sum)
    p_ortho = lax.linalg.triangular_solve(
        lower_factor, p_mean, left_side=False, lower=True, transpose_a=True
    )
    q_partial = jnp.dot(moment.T, p_ortho, precision=hp)
    q_part_rows = lax.psum_scatter(
        q_partial.astype(jnp.bfloat16), "mp", scatter_dimension=0, tiled=True
    ).astype(jnp.float32)
    q_part_rows = lax.psum(q_part_rows.astype(jnp.bfloat16), "dp").astype(jnp.float32)
    q_whole = lax.all_gather(q_part_rows, "mp", axis=0, tiled=True)
    q_factor = q_whole / replicas
    approx = jnp.dot(p_ortho, q_factor.T, precision=hp)
    new_error = (moment - approx).astype(jnp.bfloat16)[None]
    own_start = lax.axis_index("mp") * own_count
    q_own = lax.dynamic_slice_in_dim(q_factor, own_start, own_count, 0)
    return (new_error, q_own, d_attn)


def solution(mesh):
    in_specs = (
        P("dp", "mp"),
        P(("dp", "mp"), None),
        P("mp", None),
        P("dp", "mp", None),
        P("mp", None),
    )
    out_specs = (P("dp", "mp", None), P("mp", None), P("dp", "mp"))
    return jax.shard_map(
        on_device, mesh=mesh, in_specs=in_specs, out_specs=out_specs, check_vma=False
    )
```

profile of v0, /device:TPU:0, one launch (start us, length us, event | category | flops | bytes accessed | tf_op | source)
XLA Modules:
  0.0 357.0 jit_solution(13952469390451090643)
XLA Ops:
  7.2 0.0 copy-start
  7.2 0.0 all-gather.4.cloned.1.call-start
  7.2 0.7 all-gather.4.cloned.1.call-update
  7.9 0.0 all-gather.6.cloned.1.call-start
  8.0 0.7 all-gather.6.cloned.1.call-update
  8.7 0.0 reduce-scatter.2.cloned.1.call-start
  8.7 79.1 %all-gather.4.cloned.1.call-done = bf16[512,8192]{1,0:T(8,128)(2,1)} async-done(((bf16[32,8192]{1,0:T(8,128)(2,1)}), bf16[512,8192]{1,0:T(8,128)(2,1)}) %all-gather.4.cloned.1.call-update) | async-done | bytes 8388624 | tf_op jit(solution)/shard_map/all_gather | solution.py:8
  87.8 0.0 copy-done
  87.8 12.8 %convert_add_fusion = f32[512,8192]{1,0:T(8,128)} fusion(bf16[512,512]{1,0:T(8,128)(2,1)S(1)} %copy-done, bf16[512,8192]{1,0:T(8,128)(2,1)} %all-gather.4.cloned.1.call-done, bf16[1,512,8192]{2,1,0:T(8,128)(2,1)} %param.8), kind=kOutput, calls=%fused_computation | convolution fusion | flops 4303355904 | bytes 34078720 | tf_op jit(solution)/shard_map/dot_general | solution.py:9
  100.6 25.6 %all-gather.6.cloned.1.call-done = f32[8192,32]{0,1:T(8,128)} async-done(((f32[512,32]{0,1:T(8,128)}), f32[8192,32]{0,1:T(8,128)}) %all-gather.6.cloned.1.call-update) | async-done | bytes 1048592 | tf_op jit(solution)/shard_map/all_gather | solution.py:24
  126.2 18.1 %convolution_convert_fusion.2 = bf16[512,32]{0,1:T(8,128)(2,1)S(1)} fusion(f32[512,8192]{1,0:T(8,128)} %convert_add_fusion, f32[8192,32]{0,1:T(8,128)} %all-gather.6.cloned.1.call-done), kind=kOutput, calls=%fused_computation.5 | convolution fusion | flops 1610629120 | bytes 17858560 | tf_op jit(solution)/shard_map/dot_general | solution.py:28
  144.4 8.3 %psum.21 = bf16[512,32]{0,1:T(8,128)(2,1)S(1)} all-reduce(bf16[512,32]{0,1:T(8,128)(2,1)S(1)} %convolution_convert_fusion.2), channel_id=1, replica_groups=mesh['dp'=2,'mp'=16] {'dp'}, use_global_device_ids=true, to_apply=%region_0.0 | all-reduce | flops 16384 | bytes 65536 | tf_op jit(solution)/shard_map/psum | solution.py:29
  152.7 0.2 fusion.2
  152.9 57.8 %psum.22 = f32[32,32]{0,1:T(8,128)S(1)} all-reduce(f32[32,32]{0,1:T(8,128)S(1)} %fusion.2), channel_id=1, replica_groups=mesh['dp'=2,'mp'=16] {'mp'}, use_global_device_ids=true, to_apply=%region_1.0 | all-reduce | flops 1024 | bytes 8192 | tf_op jit(solution)/shard_map/psum | solution.py:30
  210.7 0.1 copy.9
  210.8 2.9 cholesky.16
  213.7 0.6 compare_reduce_fusion
  214.4 0.7 fusion.5
  215.0 2.4 custom-call.6
  217.5 0.3 fusion.1
  217.8 14.4 %convolution_convert_fusion = bf16[8192,32]{0,1:T(8,128)(2,1)} fusion(f32[512,8192]{1,0:T(8,128)} %convert_add_fusion, f32[512,32]{0,1:T(8,128)S(1)} %fusion.1), kind=kOutput, calls=%fused_computation.3 | convolution fusion | flops 1610874880 | bytes 17367040 | tf_op jit(solution)/shard_map/dot_general | solution.py:35
  232.2 0.0 reduce-scatter.2.cloned.1.call-update
  232.2 0.0 all-gather.8.cloned.1.call-start
  232.3 52.2 %reduce-scatter.2.cloned.1.call-done = bf16[512,32]{0,1:T(8,128)(2,1)} async-done(((bf16[8192,32]{0,1:T(8,128)(2,1)}), bf16[512,32]{0,1:T(8,128)(2,1)}) %reduce-scatter.2.cloned.1.call-update) | async-done | bytes 32784 | tf_op jit(solution)/shard_map/reduce_scatter | solution.py:36
  284.5 9.2 %psum.23 = bf16[512,32]{0,1:T(8,128)(2,1)S(1)} all-reduce(bf16[512,32]{0,1:T(8,128)(2,1)} %reduce-scatter.2.cloned.1.call-done), channel_id=1, replica_groups=mesh['dp'=2,'mp'=16] {'dp'}, use_global_device_ids=true, to_apply=%region_5.6 | all-reduce | flops 16384 | bytes 65536 | tf_op jit(solution)/shard_map/psum | solution.py:39
  293.7 0.6 convert_element_type.31
  294.3 0.0 all-gather.8.cloned.1.call-update
  294.3 11.1 %convolution_convert_fusion.1 = bf16[512,512]{1,0:T(8,128)(2,1)} fusion(bf16[512,8192]{1,0:T(8,128)(2,1)} %all-gather.4.cloned.1.call-done, bf16[512,8192]{1,0:T(8,128)(2,1)} %param.7), kind=kOutput, calls=%fused_computation.4 | convolution fusion | flops 4295229440 | bytes 17301504 | tf_op jit(solution)/shard_map/dot_general | solution.py:12
  305.4 25.1 %all-gather.8.cloned.1.call-done = f32[8192,32]{0,1:T(8,128)} async-done(((f32[512,32]{0,1:T(8,128)}), f32[8192,32]{0,1:T(8,128)}) %all-gather.8.cloned.1.call-update) | async-done | bytes 1048592 | tf_op jit(solution)/shard_map/all_gather | solution.py:40
  330.6 1.3 broadcast_multiply_fusion
  331.8 0.6 constant_dynamic-slice_fusion
  332.5 18.0 %fusion = bf16[1,512,8192]{2,1,0:T(8,128)(2,1)} fusion(f32[512,8192]{1,0:T(8,128)} %convert_add_fusion, f32[512,32]{0,1:T(8,128)S(1)} %fusion.1, f32[8192,32]{0,1:T(8,128)} %all-gather.8.cloned.1.call-done), kind=kOutput, calls=%fused_computation.2 | convolution fusion | flops 1619263488 | bytes 26279936 | tf_op jit(solution)/shard_map/dot_general | solution.py:42
  (2 shorter events, 0.0 us)
Async XLA Ops:
  7.2 80.6 %copy-start = (bf16[512,512]{1,0:T(8,128)(2,1)S(1)}, bf16[512,512]{1,0:T(8,128)(2,1)}, u32[]{:S(2)}) copy-start(bf16[512,512]{1,0:T(8,128)(2,1)} %param.5) | copy-start | bytes 1572868
  7.2 80.6 %all-gather.4.cloned.1.call-start = ((), (), s32[]{:S(2)}) async-start(), calls=%async_computation.1 | async-start | bytes 8912896 | tf_op jit(solution)/shard_map/all_gather | solution.py:8
  7.9 118.3 %all-gather.6.cloned.1.call-start = ((), (), s32[]{:S(2)}) async-start(), calls=%async_computation.2 | async-start | bytes 1114112 | tf_op jit(solution)/shard_map/all_gather | solution.py:24
  8.7 275.8 %reduce-scatter.2.cloned.1.call-start = ((), (), s32[]{:S(2)}) async-start(), calls=%async_computation.3 | async-start | bytes 557056 | tf_op jit(solution)/shard_map/reduce_scatter | solution.py:36
  232.2 98.3 %all-gather.8.cloned.1.call-start = ((), (), s32[]{:S(2)}) async-start(), calls=%async_computation.4 | async-start | bytes 1114112 | tf_op jit(solution)/shard_map/all_gather | solution.py:40
Sparse Core Ops, SparseCore 0:
  10.2 77.5 all-gather.3
  90.0 36.2 all-gather.5
  232.3 52.1 reduce-scatter.1
  294.5 36.0 all-gather.7
where the time goes:
time: 357 us
  waiting for transfers between devices  183 us (51%)
  blocking collectives  75.3 us (21%)
  matrix products  74.9 us (21%)
  between operations  13.8 us (4%)
  other arithmetic  8.62 us (2%)
    all_gather x1, waiting for transfers between devices, full_gradient(): piece = lax.all_gather(grad_out, 'mp', axis=0, tiled=True)  79.1 us
    psum x1, blocking collectives, on_device(): gram_sum = lax.psum(jnp.dot(p_mean.T, p_mean, precision=hp), 'mp')  57.8 us
    reduce_scatter x1, waiting for transfers between devices, on_device(): lax.psum_scatter(q_partial.astype(jnp.bfloat16), 'mp', scatter_dimension=...  52.2 us
    all_gather x1, waiting for transfers between devices, on_device(): q_full = lax.all_gather(q_start, 'mp', axis=0, tiled=True)  25.6 us
    all_gather x1, waiting for transfers between devices, on_device(): q_whole = lax.all_gather(q_part_rows, 'mp', axis=0, tiled=True)  25.1 us
    dot_general x1, matrix products, on_device(): p_local = jnp.dot(moment, q_full, precision=hp)  18.1 us
    dot_general x1, matrix products, on_device(): approx = jnp.dot(p_ortho, q_factor.T, precision=hp)  18 us
    dot_general x1, matrix products, on_device(): q_partial = jnp.dot(moment.T, p_ortho, precision=hp)  14.4 us
  transfers between devices with their start and end apart: 4, of which 4 were waited for; matrix products, arithmetic and copies ran while one was open for 7% of the time, Pallas kernels for 0%

commit v1 on v0

v1 whole, which is shorter than its diff:
```python
import functools

import jax
import jax.numpy as jnp
from jax import lax
from jax.experimental import pallas as pl
from jax.experimental.pallas import tpu as pltpu
from jax.sharding import PartitionSpec as P

MESH = pl.DeviceIdType.MESH
HP = lax.Precision.HIGHEST
F32, BF16 = jnp.float32, jnp.bfloat16
NN = (((1,), (0,)), ((), ()))
NT = (((1,), (1,)), ((), ()))
TN = (((0,), (0,)), ((), ()))
NC, NZ = 2, 4


def dot(a, b, dims, precision=None):
    return lax.dot_general(a, b, dims, precision=precision, preferred_element_type=F32)


def split(v):
    hi = v.astype(BF16)
    return hi, (v - hi.astype(F32)).astype(BF16)


def inverse_of_factor(gram):
    r = gram.shape[0]
    rows = lax.broadcasted_iota(jnp.int32, (r, 1), 0)
    eye = (rows == lax.broadcasted_iota(jnp.int32, (r, r), 1)).astype(F32)
    low, pivots = eye, jnp.ones((r, 1), F32)
    for k in range(r):
        pivot = gram[k:k + 1, k:k + 1]
        pivots = jnp.where(rows == k, pivot, pivots)
        factor = jnp.where(rows > k, gram[:, k:k + 1] / pivot, 0.0)
        low = low - factor * low[k:k + 1, :]
        gram = gram - factor * gram[k:k + 1, :]
    return low * lax.rsqrt(pivots)


def chain_kernel(n_dp, n_mp, t,
                 a_ref, g_hbm, e_hbm, q_ref,
                 gout, pp_ref, qq_ref, qown_ref,
                 e_ref, g_ref, qb, gqb, pb, sacc, gacc, qacc, qdp, q2b,
                 s1, r1, s2, r2, s3, r3, m1, m2, m3, t1, t2, t3, u1, u2, u3, gr,
                 send, recv, gsend, grecv, local):
    nx = n_mp // (NC * NZ)
    half = nx * NZ
    d, m = lax.axis_index("dp"), lax.axis_index("mp")
    c = lax.rem(m, NC)
    x = lax.rem(lax.div(m, NC), nx)
    z = lax.div(m, NC * nx)
    f = a_ref.shape[1]
    rank = q_ref.shape[1]

    def dev(zz=None, xx=None, cc=None):
        zz, xx, cc = (z if zz is None else zz), (x if xx is None else xx), (c if cc is None else cc)
        return (d, (zz * nx + xx) * NC + cc)

    def slot(zz, xx, cc):
        return (cc * nx + xx) * NZ + zz

    slots = [slot(i // (NC * nx), (i // NC) % nx, i % NC) for i in range(n_mp)]
    z_peers = [lax.rem(z + k, NZ) for k in range(1, NZ)]
    x_peers = [lax.rem(x + k, nx) for k in range(1, nx)]
    d_peers = [lax.rem(d + k, n_dp) for k in range(1, n_dp)]
    own = slot(z, x, c)

    e_copy = pltpu.make_async_copy(e_hbm.at[0], e_ref, local.at[0])
    g_copy = pltpu.make_async_copy(g_hbm, g_ref, local.at[1])
    own_rows = pl.ds(pl.multiple_of(m * t, t), t)
    o_copy = pltpu.make_async_copy(g_hbm, gout.at[own_rows, :], local.at[2])
    g_copy.start()
    e_copy.start()
    o_copy.start()

    barrier = pltpu.get_barrier_semaphore()
    for peer in ([dev(zz=p) for p in z_peers] + [dev(xx=p) for p in x_peers]
                 + [dev(cc=1 - c)] + [(p, m) for p in d_peers]):
        pl.semaphore_signal(barrier, inc=1, device_id=peer, device_id_type=MESH)
    pl.semaphore_wait(barrier, NZ + nx - 1 + n_dp - 1)

    used = [0]

    def push(src, dst, peer):
        i = used[0]
        used[0] += 1
        copy = pltpu.make_async_remote_copy(
            src_ref=src, dst_ref=dst, send_sem=send.at[i], recv_sem=recv.at[i],
            device_id=peer, device_id_type=MESH)
        copy.start()
        return copy

    def wait(copies):
        for copy in copies:
            copy.wait()

    def rows_of(zz, xx, cc):
        return pl.ds(pl.multiple_of(((zz * nx + xx) * NC + cc) * t, t), t)

    def bulk(zz, xx, cc, kind, peer, src=None):
        at = gout.at[rows_of(zz, xx, cc), :]
        i = slot(zz, xx, cc)
        return pltpu.make_async_remote_copy(
            src_ref=at if src is None else src, dst_ref=at,
            send_sem=gsend.at[kind, i], recv_sem=grecv.at[i],
            device_id=peer, device_id_type=MESH)

    k_core = 1 + nx

    def spread(zz, src=None):
        for k, p in enumerate(x_peers):
            bulk(zz, x, c, 2 + k, dev(xx=p), src).start()
        bulk(zz, x, c, k_core, dev(cc=1 - c), src).start()

    def up(zz, src=None):
        @pl.when(z < NZ - 1)
        def _():
            bulk(zz, x, c, 0, dev(zz=lax.min(z + 1, NZ - 1)), src).start()

    def down(zz, src=None):
        @pl.when(z > 0)
        def _():
            bulk(zz, x, c, 1, dev(zz=lax.max(z - 1, 0)), src).start()

    def arrived(zz, xx, cc):
        bulk(zz, xx, cc, 0, dev(cc=1 - c)).wait_recv()

    def hop(s):
        @pl.when(z >= s)
        def _():
            zz = z - s
            arrived(zz, x, c)
            up(zz)
            spread(zz)

        @pl.when(z + s < NZ)
        def _():
            zz = z + s
            arrived(zz, x, c)
            down(zz)
            spread(zz)

    def across(s):
        for p in x_peers:
            for zz, ok in ((z - s, z >= s), (z + s, z + s < NZ)):
                if s == 0:
                    ok = zz >= 0

                @pl.when(ok)
                def _(zz=zz, p=p):
                    arrived(zz, p, c)
                    bulk(zz, p, c, k_core, dev(cc=1 - c)).start()
                if s == 0:
                    break

    qb[own] = jnp.transpose(q_ref[...]).astype(BF16)
    copies = [push(qb.at[own], qb.at[own], dev(zz=p)) for p in z_peers]
    up(z, g_hbm)
    down(z, g_hbm)
    spread(z, g_hbm)
    wait(copies)
    line = pl.ds(slot(0, x, c), NZ)
    wait([push(qb.at[line], qb.at[line], dev(xx=p)) for p in x_peers])
    plane = pl.ds(slot(0, 0, c), half)
    wait([push(qb.at[plane], qb.at[plane], dev(cc=1 - c))])

    g_copy.wait()
    gq = jnp.zeros((t, rank), F32)
    for i, s in enumerate(slots):
        gq += dot(g_ref[:, i * f:(i + 1) * f], qb[s], NT)
    gqb[own] = gq
    copies = [push(gqb.at[own], gqb.at[own], dev(zz=p)) for p in z_peers]
    e_copy.wait()
    pt = jnp.zeros((rank, f), F32)
    for i, s in enumerate(slots):
        pt += dot(qb[s], e_ref[:, i * f:(i + 1) * f], NT)
    wait(copies)
    wait([push(gqb.at[line], gqb.at[line], dev(xx=p)) for p in x_peers])
    wait([push(gqb.at[plane], gqb.at[plane], dev(cc=1 - c))])
    gq_all = jnp.concatenate([gqb[s] for s in slots], axis=0)
    hi, lo = split(gq_all)
    a = a_ref[...]
    pt += dot(hi, a, TN) + dot(lo, a, TN)
    pb[d] = pt
    wait([push(pb.at[d], pb.at[d], (p, m)) for p in d_peers])
    pt = pb[0]
    for k in range(1, n_dp):
        pt += pb[k]
    pt = pt / n_dp

    p_hi, p_lo = split(pt)
    sums = dot(a, p_hi, NT) + dot(a, p_lo, NT)
    for i, s in enumerate(slots):
        sacc[s] = sums[i * t:(i + 1) * t]
    gacc[...] = dot(pt, pt, NT, HP)

    def reduce(acc, bs, br, dtype, extra):
        s_c, s_x, s_z = bs
        r_c, r_x, r_z = br
        s_c[...] = acc[pl.ds(slot(0, 0, 1 - c), half)].astype(dtype)
        copies = [push(s_c, r_c, dev(cc=1 - c))]
        if extra:
            m1[...] = gacc[...]
            copies.append(push(m1, gr.at[0], dev(cc=1 - c)))
        wait(copies)
        mine = pl.ds(slot(0, 0, c), half)
        acc[mine] = acc[mine] + r_c[...].astype(F32)
        copies = []
        if extra:
            m2[...] = gacc[...] + gr[0]
        for k, p in enumerate(x_peers):
            s_x[k] = acc[pl.ds(slot(0, p, c), NZ)].astype(dtype)
            copies.append(push(s_x.at[k], r_x.at[k], dev(xx=p)))
            if extra:
                copies.append(push(m2, gr.at[1 + k], dev(xx=p)))
        wait(copies)
        mine = pl.ds(slot(0, x, c), NZ)
        for k in range(nx - 1):
            acc[mine] = acc[mine] + r_x[k].astype(F32)
        copies = []
        if extra:
            total = m2[...]
            for k in range(nx - 1):
                total = total + gr[1 + k]
            m3[...] = total
        for k, p in enumerate(z_peers):
            s_z[k] = acc[slot(p, x, c)].astype(dtype)
            copies.append(push(s_z.at[k], r_z.at[k], dev(zz=p)))
            if extra:
                copies.append(push(m3, gr.at[nx + k], dev(zz=p)))
        wait(copies)
        out = acc[own]
        for k in range(NZ - 1):
            out = out + r_z[k].astype(F32)
        if not extra:
            return out
        total = m3[...]
        for k in range(NZ - 1):
            total = total + gr[nx + k]
        return out, total

    s_own, gram = reduce(sacc, (t1, t2, t3), (r1, r2, r3), F32, True)
    hop(1)
    across(0)

    inv = inverse_of_factor(gram)
    pot = dot(inv, pt, NN, HP)
    o_hi, o_lo = split(-pot)
    pp_ref[:rank, :] = o_hi
    pp_ref[rank:, :] = o_lo
    so_hi, so_lo = split(dot(inv, s_own, NT, HP))
    stack = jnp.concatenate([o_hi, o_lo], axis=0)
    s_stack = jnp.concatenate([so_hi, so_lo], axis=0)
    for i, s in enumerate(slots):
        cols = slice(i * f, (i + 1) * f)
        part = dot(s_stack, g_ref[:, cols], NN) - dot(stack, e_ref[:, cols], NN)
        qacc[s] = part[:rank] + part[rank:]
    hop(2)
    across(1)
    q_sum = reduce(qacc, (s1, s2, s3), (u1, u2, u3), BF16, False)
    qdp[d] = q_sum
    wait([push(qdp.at[d], qdp.at[d], (p, m)) for p in d_peers])
    q_own = qdp[0]
    for k in range(1, n_dp):
        q_own += qdp[k]
    q_own = q_own / n_dp
    qown_ref[...] = q_own
    hop(3)
    across(2)

    q2b[own] = q_own.astype(BF16)
    wait([push(q2b.at[own], q2b.at[own], dev(zz=p)) for p in z_peers])
    wait([push(q2b.at[line], q2b.at[line], dev(xx=p)) for p in x_peers])
    wait([push(q2b.at[plane], q2b.at[plane], dev(cc=1 - c))])
    for i, s in enumerate(slots):
        qq_ref[:rank, i * f:(i + 1) * f] = q2b[s]
        qq_ref[rank:, i * f:(i + 1) * f] = q2b[s]

    across(3)
    for zz in range(NZ):
        for xx in range(nx):
            arrived(zz, xx, 1 - c)
    for zz in range(NZ):
        @pl.when((zz <= z) & (z < NZ - 1))
        def _(zz=zz):
            bulk(zz, x, c, 0, dev(cc=1 - c)).wait_send()

        @pl.when((zz >= z) & (z > 0))
        def _(zz=zz):
            bulk(zz, x, c, 1, dev(cc=1 - c)).wait_send()
        for k in range(nx - 1):
            bulk(zz, x, c, 2 + k, dev(cc=1 - c)).wait_send()
        for xx in range(nx):
            bulk(zz, xx, c, k_core, dev(cc=1 - c)).wait_send()
    o_copy.wait()


def chain(n_dp, n_mp, attn_out, grad_out, error_buf, q_start):
    t, width = grad_out.shape
    tokens, f = attn_out.shape
    rank = q_start.shape[1]
    nx = n_mp // (NC * NZ)
    half = nx * NZ
    per = NZ - 1 + nx - 1 + 1
    count = 7 * per + 2 * (n_dp - 1)
    any_space = pl.BlockSpec(memory_space=pl.ANY)
    vmem = pl.BlockSpec(memory_space=pltpu.VMEM)
    other = max(nx - 1, 1)
    square = (rank, rank)
    block, tok = (rank, f), (t, rank)
    scratch = [
        pltpu.VMEM((f, width), BF16),
        pltpu.VMEM((t, width), BF16),
        pltpu.VMEM((n_mp,) + block, BF16),
        pltpu.VMEM((n_mp,) + tok, F32),
        pltpu.VMEM((n_dp,) + block, F32),
        pltpu.VMEM((n_mp,) + tok, F32),
        pltpu.VMEM(square, F32),
        pltpu.VMEM((n_mp,) + block, F32),
        pltpu.VMEM((n_dp,) + block, F32),
        pltpu.VMEM((n_mp,) + block, BF16),
        pltpu.VMEM((half,) + block, BF16),
        pltpu.VMEM((half,) + tok, F32),
        pltpu.VMEM((other, NZ) + block, BF16),
        pltpu.VMEM((other, NZ) + tok, F32),
        pltpu.VMEM((NZ - 1,) + block, BF16),
        pltpu.VMEM((NZ - 1,) + tok, F32),
        pltpu.VMEM(square, F32), pltpu.VMEM(square, F32), pltpu.VMEM(square, F32),
        pltpu.VMEM((half,) + tok, F32),
        pltpu.VMEM((other, NZ) + tok, F32),
        pltpu.VMEM((NZ - 1,) + tok, F32),
        pltpu.VMEM((half,) + block, BF16),
        pltpu.VMEM((other, NZ) + block, BF16),
        pltpu.VMEM((NZ - 1,) + block, BF16),
        pltpu.VMEM((nx + NZ - 1,) + square, F32),
        pltpu.SemaphoreType.DMA((count,)),
        pltpu.SemaphoreType.DMA((count,)),
        pltpu.SemaphoreType.DMA((2 + nx, n_mp)),
        pltpu.SemaphoreType.DMA((n_mp,)),
        pltpu.SemaphoreType.DMA((3,)),
    ]
    return pl.pallas_call(
        functools.partial(chain_kernel, n_dp, n_mp, t),
        out_shape=(
            jax.ShapeDtypeStruct((tokens, width), BF16),
            jax.ShapeDtypeStruct((2 * rank, f), BF16),
            jax.ShapeDtypeStruct((2 * rank, width), BF16),
            jax.ShapeDtypeStruct((rank, f), F32),
        ),
        in_specs=[vmem, any_space, any_space, vmem],
        out_specs=(any_space, vmem, vmem, vmem),
        scratch_shapes=scratch,
        compiler_params=pltpu.CompilerParams(
            collective_id=0, has_side_effects=True, vmem_limit_bytes=40 * 2**20),
    )(attn_out, grad_out, error_buf, q_start)


def final_kernel(a_ref, pp_ref, qown_ref, g_ref, w_ref, e_ref, qq_ref,
                 err_ref, q_ref, da_ref, lhs, acc):
    j = pl.program_id(0)
    tokens = a_ref.shape[0]

    @pl.when(j == 0)
    def _():
        lhs[:, :tokens] = jnp.transpose(a_ref[...])
        lhs[:, tokens:] = jnp.transpose(pp_ref[...])
        q_ref[...] = jnp.transpose(qown_ref[...])
        acc[...] = jnp.zeros_like(acc)

    g = g_ref[...]
    moment = dot(lhs[:, :tokens], g, NN) + e_ref[0].astype(F32)
    err_ref[0] = (moment + dot(lhs[:, tokens:], qq_ref[...], NN)).astype(BF16)
    acc[...] += dot(g, w_ref[...], NT)

    @pl.when(j == pl.num_programs(0) - 1)
    def _():
        da_ref[...] = acc[...].astype(BF16)


def final(attn_out, pp, qown, g_all, proj_weight, error_buf, qq):
    tokens, f = attn_out.shape
    width = g_all.shape[1]
    rank = qown.shape[0]
    n = 1024
    whole = lambda shape: pl.BlockSpec(shape, lambda j: (0,) * len(shape))
    cols = lambda rows: pl.BlockSpec((rows, n), lambda j: (0, j))
    cols3 = pl.BlockSpec((1, f, n), lambda j: (0, 0, j))
    return pl.pallas_call(
        final_kernel,
        grid=(width // n,),
        out_shape=(
            jax.ShapeDtypeStruct((1, f, width), BF16),
            jax.ShapeDtypeStruct((f, rank), F32),
            jax.ShapeDtypeStruct((tokens, f), BF16),
        ),
        in_specs=[whole((tokens, f)), whole((2 * rank, f)), whole((rank, f)),
                  cols(tokens), cols(f), cols3, cols(2 * rank)],
        out_specs=(cols3, whole((f, rank)), whole((tokens, f))),
        scratch_shapes=[pltpu.VMEM((f, tokens + 2 * rank), BF16), pltpu.VMEM((tokens, f), F32)],
        compiler_params=pltpu.CompilerParams(vmem_limit_bytes=40 * 2**20),
    )(attn_out, pp, qown, g_all, proj_weight, error_buf, qq)


def on_device(n_dp, n_mp, attn_out, grad_out, proj_weight, error_buf, q_start):
    g_all, pp, qq, qown = chain(n_dp, n_mp, attn_out, grad_out, error_buf, q_start)
    return final(attn_out, pp, qown, g_all, proj_weight, error_buf, qq)


def solution(mesh):
    in_specs = (
        P("dp", "mp"),
        P(("dp", "mp"), None),
        P("mp", None),
        P("dp", "mp", None),
        P("mp", None),
    )
    out_specs = (P("dp", "mp", None), P("mp", None), P("dp", "mp"))
    return jax.shard_map(
        functools.partial(on_device, mesh.shape["dp"], mesh.shape["mp"]),
        mesh=mesh, in_specs=in_specs, out_specs=out_specs, check_vma=False,
    )
```

time: 357 us -> 128 us (0.36)
  waiting for transfers between devices: 183 us -> 0 us
  Pallas kernels: 0 us -> 123 us
  blocking collectives: 75.3 us -> 0 us
  matrix products: 74.9 us -> 0 us
  between operations: 13.8 us -> 0.66 us
  other arithmetic: 8.62 us -> 0 us
    all_gather x3 -> x0, waiting for transfers between devices: 130 us -> none  [the longest x1 79.1 us: full_gradient(): piece = lax.all_gather(grad_out, 'mp', axis=0, tiled=True)]
    pallas_call x0 -> x2, Pallas kernels: none -> 123 us  [the longest x1 106 us: chain(): pl.pallas_call(functools.partial(chain_kernel, n_dp, n_mp, t), out_shape=...]
    psum x3 -> x0, blocking collectives: 75.3 us -> none  [the longest x1 57.8 us: on_device(): gram_sum = lax.psum(jnp.dot(p_mean.T, p_mean, precision=hp), 'mp')]
    dot_general x6 -> x0, matrix products: 74.6 us -> none  [the longest x1 18.1 us: on_device(): p_local = jnp.dot(moment, q_full, precision=hp)]
    reduce_scatter x1 -> x0, waiting for transfers between devices: 52.2 us -> none  [on_device(): lax.psum_scatter(q_partial.astype(jnp.bfloat16), 'mp', scatter_dimension=...]
    another operation x5 -> x0, other arithmetic: 6.68 us -> none  [the longest x3 3.59 us: on_device(): lower_factor = jnp.linalg.cholesky(gram_sum)]
  transfers between devices with their start and end apart: 4 -> 0, of which waited for: 4 -> 0; matrix products, arithmetic and copies ran while one was open for 7% -> 0% of each run, Pallas kernels for 0% -> 0%
where the time goes in v1:
time: 128 us; the launch traced here: 127 us
  Pallas kernels  123 us (96%)
  local copies, waits for them, and re-layouts  3.78 us (3%)
    pallas_call x1, Pallas kernels, chain(): pl.pallas_call(functools.partial(chain_kernel, n_dp, n_mp, t), out_shape=...  106 us
    pallas_call x1, Pallas kernels, final(): pl.pallas_call(final_kernel, grid=(width // n,), out_shape=(jax.ShapeDtyp...  16.8 us
    unnamed x5, local copies, waits for them, and re-layouts  3.04 us

profile of v1, /device:TPU:0, one launch (start us, length us, event | category | flops | bytes accessed | tf_op | source)
XLA Modules:
  0.0 127.4 jit_solution(16481363742225646551)
XLA Ops:
  0.6 1.0 copy.8.q_ref
  1.6 0.0 copy-start
  1.6 1.0 copy-done
  2.6 0.0 copy-start.1
  2.6 1.0 copy-done.1
  3.7 106.2 %shard_map.76 = (bf16[512,8192]{1,0:T(8,128)(2,1)S(1)}, bf16[64,512]{1,0:T(8,128)(2,1)S(1)}, bf16[64,8192]{1,0:T(8,128)(2,1)S(1)}, f32[32,512]{1,0:T(8,128)S(1)}) custom-call(bf16[512,512]{1,0:T(8,128)(2,1)S(1)} %copy-done, bf16[32,8192]{1,0:T(8,128)(2,1)S(1)} %copy-done.1, bf16[1,512,8192]{2,1,0:T(8,128)(2,1)} %e_ref.1, f32[512,32]{1,0:T(8,128)S(1)} %copy.8.q_ref), custom_call_target="tpu_custom_call" | custom-call | tf_op jit(solution)/shard_map/pallas_call | solution.py:344
  109.8 16.8 %shard_map.77 = (bf16[1,512,8192]{2,1,0:T(8,128)(2,1)}, f32[512,32]{1,0:T(8,128)S(1)}, bf16[512,512]{1,0:T(8,128)(2,1)}) custom-call(bf16[512,512]{1,0:T(8,128)(2,1)S(1)} %copy-done, bf16[64,512]{1,0:T(8,128)(2,1)S(1)} %get-tuple-element.7.pp_ref, f32[32,512]{1,0:T(8,128)S(1)} %get-tuple-element.8.qown_ref, bf16[512,8192]{1,0:T(8,128)(2,1)S(1)} %get-tuple-element.9.g_ref, ...), custom_call_target="tpu_custom_call" | custom-call | tf_op jit(solution)/shard_map/pallas_call | solution.py:390
  126.6 0.7 copy.9
Async XLA Ops:
  1.6 1.0 copy-start
  2.6 1.0 copy-start.1

commit v2 on v1

--- a/solution.py
+++ b/solution.py
@@ -42,8 +42,7 @@
 def chain_kernel(n_dp, n_mp, t,
                  a_ref, g_hbm, e_hbm, q_ref,
                  gout, pp_ref, qq_ref, qown_ref,
-                 e_ref, g_ref, qb, gqb, pb, sacc, gacc, qacc, qdp, q2b,
-                 s1, r1, s2, r2, s3, r3, m1, m2, m3, t1, t2, t3, u1, u2, u3, gr,
+                 e_ref, g_ref, qb, gqb, pb, sx, rx, qacc, qdp, q2b, s1, u1, s2, u2,
                  send, recv, gsend, grecv, local):
     nx = n_mp // (NC * NZ)
     half = nx * NZ
@@ -52,7 +51,7 @@
     x = lax.rem(lax.div(m, NC), nx)
     z = lax.div(m, NC * nx)
     f = a_ref.shape[1]
-    rank = q_ref.shape[1]
+    rank = q_ref.shape[0]
 
     def dev(zz=None, xx=None, cc=None):
         zz, xx, cc = (z if zz is None else zz), (x if xx is None else xx), (c if cc is None else cc)
@@ -62,7 +61,6 @@
         return (cc * nx + xx) * NZ + zz
 
     slots = [slot(i // (NC * nx), (i // NC) % nx, i % NC) for i in range(n_mp)]
-    z_peers = [lax.rem(z + k, NZ) for k in range(1, NZ)]
     x_peers = [lax.rem(x + k, nx) for k in range(1, nx)]
     d_peers = [lax.rem(d + k, n_dp) for k in range(1, n_dp)]
     own = slot(z, x, c)
@@ -76,10 +74,11 @@
     o_copy.start()
 
     barrier = pltpu.get_barrier_semaphore()
-    for peer in ([dev(zz=p) for p in z_peers] + [dev(xx=p) for p in x_peers]
-                 + [dev(cc=1 - c)] + [(p, m) for p in d_peers]):
-        pl.semaphore_signal(barrier, inc=1, device_id=peer, device_id_type=MESH)
-    pl.semaphore_wait(barrier, NZ + nx - 1 + n_dp - 1)
+    for k in range(1, n_mp):
+        pl.semaphore_signal(barrier, inc=1, device_id=(d, lax.rem(m + k, n_mp)), device_id_type=MESH)
+    for p in d_peers:
+        pl.semaphore_signal(barrier, inc=1, device_id=(p, m), device_id_type=MESH)
+    pl.semaphore_wait(barrier, n_mp - 1 + n_dp - 1)
 
     used = [0]
 
@@ -155,31 +154,62 @@
                 if s == 0:
                     break
 
-    qb[own] = jnp.transpose(q_ref[...]).astype(BF16)
-    copies = [push(qb.at[own], qb.at[own], dev(zz=p)) for p in z_peers]
+    def plane_peers():
+        out = []
+        for kx in range(nx):
+            for kz in range(NZ):
+                if kx or kz:
+                    out.append((lax.rem(z + kz, NZ), lax.rem(x + kx, nx)))
+        return out
+
+    chips = plane_peers()
+    back = [(lax.rem(z + NZ - kz, NZ), lax.rem(x + nx - kx, nx))
+            for kx in range(nx) for kz in range(NZ) if kx or kz]
+
+    def gather_start(buf):
+        copies = [push(buf.at[own], buf.at[own], dev(zz=zz, xx=xx)) for zz, xx in chips]
+        return copies, [push(buf.at[own], buf.at[own], dev(cc=1 - c))]
+
+    def gather_end(buf, copies, core):
+        for copy, (zz, xx) in zip(copies, back):
+            copy.wait_recv()
+            at = slot(zz, xx, c)
+            core.append(push(buf.at[at], buf.at[at], dev(cc=1 - c)))
+        for copy in copies:
+            copy.wait_send()
+        wait(core)
+
+    def all_peers():
+        return [lax.rem(m + k, n_mp) for k in range(1, n_mp)]
+
+    def pack(v):
+        n = v.shape[0] * rank // 128
+        return jnp.concatenate([v[k * n:(k + 1) * n] for k in range(128 // rank)], axis=1)
+
+    def unpack(v):
+        return jnp.concatenate([v[:, k * rank:(k + 1) * rank] for k in range(128 // rank)], axis=0)
+
+    qb[own] = q_ref[...].astype(BF16)
+    copies, core = gather_start(qb)
     up(z, g_hbm)
     down(z, g_hbm)
     spread(z, g_hbm)
-    wait(copies)
-    line = pl.ds(slot(0, x, c), NZ)
-    wait([push(qb.at[line], qb.at[line], dev(xx=p)) for p in x_peers])
-    plane = pl.ds(slot(0, 0, c), half)
-    wait([push(qb.at[plane], qb.at[plane], dev(cc=1 - c))])
+    gather_end(qb, copies, core)
 
     g_copy.wait()
     gq = jnp.zeros((t, rank), F32)
     for i, s in enumerate(slots):
         gq += dot(g_ref[:, i * f:(i + 1) * f], qb[s], NT)
-    gqb[own] = gq
-    copies = [push(gqb.at[own], gqb.at[own], dev(zz=p)) for p in z_peers]
+    gqb[m] = pack(gq)
+    copies = [push(gqb.at[m], gqb.at[m], (d, p)) for p in all_peers()]
     e_copy.wait()
     pt = jnp.zeros((rank, f), F32)
     for i, s in enumerate(slots):
         pt += dot(qb[s], e_ref[:, i * f:(i + 1) * f], NT)
+    hop(1)
+    across(0)
     wait(copies)
-    wait([push(gqb.at[line], gqb.at[line], dev(xx=p)) for p in x_peers])
-    wait([push(gqb.at[plane], gqb.at[plane], dev(cc=1 - c))])
-    gq_all = jnp.concatenate([gqb[s] for s in slots], axis=0)
+    gq_all = jnp.concatenate([unpack(gqb[i]) for i in range(n_mp)], axis=0)
     hi, lo = split(gq_all)
     a = a_ref[...]
     pt += dot(hi, a, TN) + dot(lo, a, TN)
@@ -192,58 +222,20 @@
 
     p_hi, p_lo = split(pt)
     sums = dot(a, p_hi, NT) + dot(a, p_lo, NT)
-    for i, s in enumerate(slots):
-        sacc[s] = sums[i * t:(i + 1) * t]
-    gacc[...] = dot(pt, pt, NT, HP)
-
-    def reduce(acc, bs, br, dtype, extra):
-        s_c, s_x, s_z = bs
-        r_c, r_x, r_z = br
-        s_c[...] = acc[pl.ds(slot(0, 0, 1 - c), half)].astype(dtype)
-        copies = [push(s_c, r_c, dev(cc=1 - c))]
-        if extra:
-            m1[...] = gacc[...]
-            copies.append(push(m1, gr.at[0], dev(cc=1 - c)))
-        wait(copies)
-        mine = pl.ds(slot(0, 0, c), half)
-        acc[mine] = acc[mine] + r_c[...].astype(F32)
-        copies = []
-        if extra:
-            m2[...] = gacc[...] + gr[0]
-        for k, p in enumerate(x_peers):
-            s_x[k] = acc[pl.ds(slot(0, p, c), NZ)].astype(dtype)
-            copies.append(push(s_x.at[k], r_x.at[k], dev(xx=p)))
-            if extra:
-                copies.append(push(m2, gr.at[1 + k], dev(xx=p)))
-        wait(copies)
-        mine = pl.ds(slot(0, x, c), NZ)
-        for k in range(nx - 1):
-            acc[mine] = acc[mine] + r_x[k].astype(F32)
-        copies = []
-        if extra:
-            total = m2[...]
-            for k in range(nx - 1):
-                total = total + gr[1 + k]
-            m3[...] = total
-        for k, p in enumerate(z_peers):
-            s_z[k] = acc[slot(p, x, c)].astype(dtype)
-            copies.append(push(s_z.at[k], r_z.at[k], dev(zz=p)))
-            if extra:
-                copies.append(push(m3, gr.at[nx + k], dev(zz=p)))
-        wait(copies)
-        out = acc[own]
-        for k in range(NZ - 1):
-            out = out + r_z[k].astype(F32)
-        if not extra:
-            return out
-        total = m3[...]
-        for k in range(NZ - 1):
-            total = total + gr[nx + k]
-        return out, total
-
-    s_own, gram = reduce(sacc, (t1, t2, t3), (r1, r2, r3), F32, True)
-    hop(1)
-    across(0)
+    gram = pack(dot(pt, pt, NT, HP))
+    nt = t * rank // 128
+    for i in range(n_mp):
+        sx[i, :nt] = pack(sums[i * t:(i + 1) * t])
+        sx[i, nt:] = gram
+    rx[m] = sx[m]
+    copies = [push(sx.at[p], rx.at[m], (d, p)) for p in all_peers()]
+    hop(2)
+    across(1)
+    wait(copies)
+    total = rx[0]
+    for i in range(1, n_mp):
+        total += rx[i]
+    s_own, gram = unpack(total[:nt]), unpack(total[nt:])
 
     inv = inverse_of_factor(gram)
     pot = dot(inv, pt, NN, HP)
@@ -253,13 +245,34 @@
     so_hi, so_lo = split(dot(inv, s_own, NT, HP))
     stack = jnp.concatenate([o_hi, o_lo], axis=0)
     s_stack = jnp.concatenate([so_hi, so_lo], axis=0)
-    for i, s in enumerate(slots):
-        cols = slice(i * f, (i + 1) * f)
-        part = dot(s_stack, g_ref[:, cols], NN) - dot(stack, e_ref[:, cols], NN)
-        qacc[s] = part[:rank] + part[rank:]
-    hop(2)
-    across(1)
-    q_sum = reduce(qacc, (s1, s2, s3), (u1, u2, u3), BF16, False)
+
+    def part(zz, xx, cc):
+        cols = pl.ds(pl.multiple_of(((zz * nx + xx) * NC + cc) * f, f), f)
+        v = dot(s_stack, g_ref[:, cols], NN) - dot(stack, e_ref[:, cols], NN)
+        return v[:rank] + v[rank:]
+
+    copies = []
+    for xx in range(nx):
+        for zz in range(NZ):
+            k = xx * NZ + zz
+            s1[k] = part(zz, xx, 1 - c).astype(BF16)
+            copies.append(push(s1.at[k], u1.at[k], dev(cc=1 - c)))
+    for xx in range(nx):
+        for zz in range(NZ):
+            qacc[xx * NZ + zz] = part(zz, xx, c)
+    wait(copies)
+    copies = []
+    for k, (zz, xx) in enumerate(chips):
+        at = xx * NZ + zz
+        s2[k] = (qacc[at] + u1[at].astype(F32)).astype(BF16)
+        copies.append(push(s2.at[k], u2.at[k], dev(zz=zz, xx=xx)))
+    at = x * NZ + z
+    q_sum = qacc[at] + u1[at].astype(F32)
+    hop(3)
+    across(2)
+    wait(copies)
+    for k in range(len(chips)):
+        q_sum += u2[k].astype(F32)
     qdp[d] = q_sum
     wait([push(qdp.at[d], qdp.at[d], (p, m)) for p in d_peers])
     q_own = qdp[0]
@@ -267,18 +280,15 @@
         q_own += qdp[k]
     q_own = q_own / n_dp
     qown_ref[...] = q_own
-    hop(3)
-    across(2)
 
     q2b[own] = q_own.astype(BF16)
-    wait([push(q2b.at[own], q2b.at[own], dev(zz=p)) for p in z_peers])
-    wait([push(q2b.at[line], q2b.at[line], dev(xx=p)) for p in x_peers])
-    wait([push(q2b.at[plane], q2b.at[plane], dev(cc=1 - c))])
+    copies, core = gather_start(q2b)
+    across(3)
+    gather_end(q2b, copies, core)
     for i, s in enumerate(slots):
         qq_ref[:rank, i * f:(i + 1) * f] = q2b[s]
         qq_ref[rank:, i * f:(i + 1) * f] = q2b[s]
 
-    across(3)
     for zz in range(NZ):
         for xx in range(nx):
             arrived(zz, xx, 1 - c)
@@ -300,41 +310,29 @@
 def chain(n_dp, n_mp, attn_out, grad_out, error_buf, q_start):
     t, width = grad_out.shape
     tokens, f = attn_out.shape
-    rank = q_start.shape[1]
+    rank = q_start.shape[0]
     nx = n_mp // (NC * NZ)
     half = nx * NZ
-    per = NZ - 1 + nx - 1 + 1
-    count = 7 * per + 2 * (n_dp - 1)
+    count = 2 * (2 * half - 1) + 2 * (n_mp - 1) + (2 * half - 1) + 2 * (n_dp - 1)
+    nt, ng = t * rank // 128, rank * rank // 128
     any_space = pl.BlockSpec(memory_space=pl.ANY)
     vmem = pl.BlockSpec(memory_space=pltpu.VMEM)
-    other = max(nx - 1, 1)
-    square = (rank, rank)
-    block, tok = (rank, f), (t, rank)
+    block = (rank, f)
     scratch = [
         pltpu.VMEM((f, width), BF16),
         pltpu.VMEM((t, width), BF16),
         pltpu.VMEM((n_mp,) + block, BF16),
-        pltpu.VMEM((n_mp,) + tok, F32),
+        pltpu.VMEM((n_mp, nt, 128), F32),
         pltpu.VMEM((n_dp,) + block, F32),
-        pltpu.VMEM((n_mp,) + tok, F32),
-        pltpu.VMEM(square, F32),
-        pltpu.VMEM((n_mp,) + block, F32),
+        pltpu.VMEM((n_mp, nt + ng, 128), F32),
+        pltpu.VMEM((n_mp, nt + ng, 128), F32),
+        pltpu.VMEM((half,) + block, F32),
         pltpu.VMEM((n_dp,) + block, F32),
         pltpu.VMEM((n_mp,) + block, BF16),
         pltpu.VMEM((half,) + block, BF16),
-        pltpu.VMEM((half,) + tok, F32),
-        pltpu.VMEM((other, NZ) + block, BF16),
-        pltpu.VMEM((other, NZ) + tok, F32),
-        pltpu.VMEM((NZ - 1,) + block, BF16),
-        pltpu.VMEM((NZ - 1,) + tok, F32),
-        pltpu.VMEM(square, F32), pltpu.VMEM(square, F32), pltpu.VMEM(square, F32),
-        pltpu.VMEM((half,) + tok, F32),
-        pltpu.VMEM((other, NZ) + tok, F32),
-        pltpu.VMEM((NZ - 1,) + tok, F32),
         pltpu.VMEM((half,) + block, BF16),
-        pltpu.VMEM((other, NZ) + block, BF16),
-        pltpu.VMEM((NZ - 1,) + block, BF16),
-        pltpu.VMEM((nx + NZ - 1,) + square, F32),
+        pltpu.VMEM((half - 1,) + block, BF16),
+        pltpu.VMEM((half - 1,) + block, BF16),
         pltpu.SemaphoreType.DMA((count,)),
         pltpu.SemaphoreType.DMA((count,)),
         pltpu.SemaphoreType.DMA((2 + nx, n_mp)),
@@ -366,7 +364,7 @@
     def _():
         lhs[:, :tokens] = jnp.transpose(a_ref[...])
         lhs[:, tokens:] = jnp.transpose(pp_ref[...])
-        q_ref[...] = jnp.transpose(qown_ref[...])
+        q_ref[...] = qown_ref[...]
         acc[...] = jnp.zeros_like(acc)
 
     g = g_ref[...]
@@ -392,20 +390,21 @@
         grid=(width // n,),
         out_shape=(
             jax.ShapeDtypeStruct((1, f, width), BF16),
-            jax.ShapeDtypeStruct((f, rank), F32),
+            jax.ShapeDtypeStruct((rank, f), F32),
             jax.ShapeDtypeStruct((tokens, f), BF16),
         ),
         in_specs=[whole((tokens, f)), whole((2 * rank, f)), whole((rank, f)),
                   cols(tokens), cols(f), cols3, cols(2 * rank)],
-        out_specs=(cols3, whole((f, rank)), whole((tokens, f))),
+        out_specs=(cols3, whole((rank, f)), whole((tokens, f))),
         scratch_shapes=[pltpu.VMEM((f, tokens + 2 * rank), BF16), pltpu.VMEM((tokens, f), F32)],
         compiler_params=pltpu.CompilerParams(vmem_limit_bytes=40 * 2**20),
     )(attn_out, pp, qown, g_all, proj_weight, error_buf, qq)
 
 
 def on_device(n_dp, n_mp, attn_out, grad_out, proj_weight, error_buf, q_start):
-    g_all, pp, qq, qown = chain(n_dp, n_mp, attn_out, grad_out, error_buf, q_start)
-    return final(attn_out, pp, qown, g_all, proj_weight, error_buf, qq)
+    g_all, pp, qq, qown = chain(n_dp, n_mp, attn_out, grad_out, error_buf, q_start.T)
+    err, q_t, d_attn = final(attn_out, pp, qown, g_all, proj_weight, error_buf, qq)
+    return err, q_t.T, d_attn
 
 
 def solution(mesh):

time: 128 us -> 97.9 us (0.76)
  Pallas kernels: 123 us -> 93.8 us
    pallas_call x1, Pallas kernels: 106 us -> 77 us  [chain(): pl.pallas_call(functools.partial(chain_kernel, n_dp, n_mp, t), out_shape=...]
    unnamed x5 -> x6, local copies, waits for them, and re-layouts: 3.04 us -> 2.91 us
where the time goes in v2:
time: 97.9 us; the launch traced here: 97.4 us
  Pallas kernels  93.8 us (96%)
  local copies, waits for them, and re-layouts  2.91 us (3%)
    pallas_call x1, Pallas kernels, chain(): pl.pallas_call(functools.partial(chain_kernel, n_dp, n_mp, t), out_shape=...  77 us
    pallas_call x1, Pallas kernels, final(): pl.pallas_call(final_kernel, grid=(width // n,), out_shape=(jax.ShapeDtyp...  16.8 us
    unnamed x6, local copies, waits for them, and re-layouts  2.91 us

profile of v2, /device:TPU:0, one launch (start us, length us, event | category | flops | bytes accessed | tf_op | source)
XLA Modules:
  0.0 97.4 jit_solution(14532647962360012469)
XLA Ops:
  0.6 0.0 copy-start
  0.6 1.0 %copy-done = bf16[512,512]{1,0:T(8,128)(2,1)S(1)} copy-done((bf16[512,512]{1,0:T(8,128)(2,1)S(1)}, bf16[512,512]{1,0:T(8,128)(2,1)}, u32[]{:S(2)}) %copy-start) | copy-done | bytes 524312
  1.7 0.0 copy-start.1
  1.7 1.0 %copy-done.1 = bf16[32,8192]{1,0:T(8,128)(2,1)S(1)} copy-done((bf16[32,8192]{1,0:T(8,128)(2,1)S(1)}, bf16[32,8192]{1,0:T(8,128)(2,1)}, u32[]{:S(2)}) %copy-start.1) | copy-done | bytes 524312
  2.7 0.0 copy-start.2
  2.7 0.8 copy-done.2
  3.6 77.0 %shard_map.76 = (bf16[512,8192]{1,0:T(8,128)(2,1)S(1)}, bf16[64,512]{1,0:T(8,128)(2,1)S(1)}, bf16[64,8192]{1,0:T(8,128)(2,1)S(1)}, f32[32,512]{1,0:T(8,128)S(1)}) custom-call(bf16[512,512]{1,0:T(8,128)(2,1)S(1)} %copy-done, bf16[32,8192]{1,0:T(8,128)(2,1)S(1)} %copy-done.1, bf16[1,512,8192]{2,1,0:T(8,128)(2,1)} %e_ref.1, f32[32,512]{1,0:T(8,128)S(1)} %bitcast.2), custom_call_target="tpu_custom_call" | custom-call | tf_op jit(solution)/shard_map/pallas_call | solution.py:342
  80.6 16.8 %shard_map.77 = (bf16[1,512,8192]{2,1,0:T(8,128)(2,1)}, f32[32,512]{1,0:T(8,128)}, bf16[512,512]{1,0:T(8,128)(2,1)}) custom-call(bf16[512,512]{1,0:T(8,128)(2,1)S(1)} %copy-done, bf16[64,512]{1,0:T(8,128)(2,1)S(1)} %get-tuple-element.10.pp_ref, f32[32,512]{1,0:T(8,128)S(1)} %get-tuple-element.11.qown_ref, bf16[512,8192]{1,0:T(8,128)(2,1)S(1)} %get-tuple-element.12.g_ref, ...), custom_call_target="tpu_custom_call" | custom-call | tf_op jit(solution)/shard_map/pallas_call | solution.py:388
Async XLA Ops:
  0.6 1.0 %copy-start = (bf16[512,512]{1,0:T(8,128)(2,1)S(1)}, bf16[512,512]{1,0:T(8,128)(2,1)}, u32[]{:S(2)}) copy-start(bf16[512,512]{1,0:T(8,128)(2,1)} %a_ref.3) | copy-start | bytes 1572868
  1.7 1.0 %copy-start.1 = (bf16[32,8192]{1,0:T(8,128)(2,1)S(1)}, bf16[32,8192]{1,0:T(8,128)(2,1)}, u32[]{:S(2)}) copy-start(bf16[32,8192]{1,0:T(8,128)(2,1)} %g_hbm.1) | copy-start | bytes 1572868
  2.7 0.8 copy-start.2

commit v3 on v2

--- a/solution.py
+++ b/solution.py
@@ -40,9 +40,9 @@
 
 
 def chain_kernel(n_dp, n_mp, t,
-                 a_ref, g_hbm, e_hbm, q_ref,
-                 gout, pp_ref, qq_ref, qown_ref,
-                 e_ref, g_ref, qb, gqb, pb, sx, rx, qacc, qdp, q2b, s1, u1, s2, u2,
+                 a_hbm, g_hbm, e_hbm, w_hbm, q_ref,
+                 gout, lhs_ref, qq_ref, qown_ref, da_ref,
+                 a_ref, e_ref, w_ref, grp, g_ref, qb, gqb, pb, sx, rx, qacc, qdp, q2b, s1, u1, s2, u2,
                  send, recv, gsend, grecv, local):
     nx = n_mp // (NC * NZ)
     half = nx * NZ
@@ -69,9 +69,13 @@
     g_copy = pltpu.make_async_copy(g_hbm, g_ref, local.at[1])
     own_rows = pl.ds(pl.multiple_of(m * t, t), t)
     o_copy = pltpu.make_async_copy(g_hbm, gout.at[own_rows, :], local.at[2])
+    a_copy = pltpu.make_async_copy(a_hbm, a_ref, local.at[3])
+    w_copy = pltpu.make_async_copy(w_hbm, w_ref, local.at[4])
     g_copy.start()
     e_copy.start()
+    a_copy.start()
     o_copy.start()
+    w_copy.start()
 
     barrier = pltpu.get_barrier_semaphore()
     for k in range(1, n_mp):
@@ -188,6 +192,26 @@
 
     def unpack(v):
         return jnp.concatenate([v[:, k * rank:(k + 1) * rank] for k in range(128 // rank)], axis=0)
+
+    tz = nx * NC * t
+
+    def group_rows(k):
+        return pl.ds(pl.multiple_of(lax.rem(z + k, NZ) * tz, tz), tz)
+
+    def group_load(k):
+        zz = lax.rem(z + k, NZ)
+        for xx in range(nx):
+            arrived(zz, xx, 1 - c)
+        copy = pltpu.make_async_copy(gout.at[group_rows(k), :], grp.at[k], local.at[5 + k])
+        copy.start()
+        return copy
+
+    def group_dot(k, copy):
+        copy.wait()
+        v = jnp.zeros((tz, f), F32)
+        for i in range(0, w_ref.shape[1], 512):
+            v += dot(grp[k, :, i:i + 512], w_ref[:, i:i + 512], NT)
+        da_ref[group_rows(k), :] = v.astype(BF16)
 
     qb[own] = q_ref[...].astype(BF16)
     copies, core = gather_start(qb)
@@ -211,6 +235,7 @@
     wait(copies)
     gq_all = jnp.concatenate([unpack(gqb[i]) for i in range(n_mp)], axis=0)
     hi, lo = split(gq_all)
+    a_copy.wait()
     a = a_ref[...]
     pt += dot(hi, a, TN) + dot(lo, a, TN)
     pb[d] = pt
@@ -229,8 +254,13 @@
         sx[i, nt:] = gram
     rx[m] = sx[m]
     copies = [push(sx.at[p], rx.at[m], (d, p)) for p in all_peers()]
+    o_copy.wait()
+    w_copy.wait()
+    loaded = group_load(0)
     hop(2)
     across(1)
+    group_dot(0, loaded)
+    lhs_ref[:, :a_ref.shape[0]] = jnp.transpose(a_ref[...])
     wait(copies)
     total = rx[0]
     for i in range(1, n_mp):
@@ -240,8 +270,6 @@
     inv = inverse_of_factor(gram)
     pot = dot(inv, pt, NN, HP)
     o_hi, o_lo = split(-pot)
-    pp_ref[:rank, :] = o_hi
-    pp_ref[rank:, :] = o_lo
     so_hi, so_lo = split(dot(inv, s_own, NT, HP))
     stack = jnp.concatenate([o_hi, o_lo], axis=0)
     s_stack = jnp.concatenate([so_hi, so_lo], axis=0)
@@ -270,11 +298,16 @@
     q_sum = qacc[at] + u1[at].astype(F32)
     hop(3)
     across(2)
+    across(3)
+    loaded = [group_load(k) for k in range(1, NZ)]
+    group_dot(1, loaded[0])
     wait(copies)
     for k in range(len(chips)):
         q_sum += u2[k].astype(F32)
     qdp[d] = q_sum
-    wait([push(qdp.at[d], qdp.at[d], (p, m)) for p in d_peers])
+    copies = [push(qdp.at[d], qdp.at[d], (p, m)) for p in d_peers]
+    group_dot(2, loaded[1])
+    wait(copies)
     q_own = qdp[0]
     for k in range(1, n_dp):
         q_own += qdp[k]
@@ -283,15 +316,13 @@
 
     q2b[own] = q_own.astype(BF16)
     copies, core = gather_start(q2b)
-    across(3)
+    lhs_ref[:, a_ref.shape[0]:] = jnp.transpose(stack)
+    group_dot(3, loaded[2])
     gather_end(q2b, copies, core)
     for i, s in enumerate(slots):
         qq_ref[:rank, i * f:(i + 1) * f] = q2b[s]
         qq_ref[rank:, i * f:(i + 1) * f] = q2b[s]
 
-    for zz in range(NZ):
-        for xx in range(nx):
-            arrived(zz, xx, 1 - c)
     for zz in range(NZ):
         @pl.when((zz <= z) & (z < NZ - 1))
         def _(zz=zz):
@@ -304,10 +335,9 @@
             bulk(zz, x, c, 2 + k, dev(cc=1 - c)).wait_send()
         for xx in range(nx):
             bulk(zz, xx, c, k_core, dev(cc=1 - c)).wait_send()
-    o_copy.wait()
-
-
-def chain(n_dp, n_mp, attn_out, grad_out, error_buf, q_start):
+
+
+def chain(n_dp, n_mp, attn_out, grad_out, error_buf, proj_weight, q_start):
     t, width = grad_out.shape
     tokens, f = attn_out.shape
     rank = q_start.shape[0]
@@ -319,7 +349,10 @@
     vmem = pl.BlockSpec(memory_space=pltpu.VMEM)
     block = (rank, f)
     scratch = [
+        pltpu.VMEM((tokens, f), BF16),
         pltpu.VMEM((f, width), BF16),
+        pltpu.VMEM((f, width), BF16),
+        pltpu.VMEM((NZ, tokens // NZ, width), BF16),
         pltpu.VMEM((t, width), BF16),
         pltpu.VMEM((n_mp,) + block, BF16),
         pltpu.VMEM((n_mp, nt, 128), F32),
@@ -337,50 +370,40 @@
         pltpu.SemaphoreType.DMA((count,)),
         pltpu.SemaphoreType.DMA((2 + nx, n_mp)),
         pltpu.SemaphoreType.DMA((n_mp,)),
-        pltpu.SemaphoreType.DMA((3,)),
+        pltpu.SemaphoreType.DMA((5 + NZ,)),
     ]
     return pl.pallas_call(
         functools.partial(chain_kernel, n_dp, n_mp, t),
         out_shape=(
             jax.ShapeDtypeStruct((tokens, width), BF16),
-            jax.ShapeDtypeStruct((2 * rank, f), BF16),
+            jax.ShapeDtypeStruct((f, tokens + 2 * rank), BF16),
             jax.ShapeDtypeStruct((2 * rank, width), BF16),
             jax.ShapeDtypeStruct((rank, f), F32),
+            jax.ShapeDtypeStruct((tokens, f), BF16),
         ),
-        in_specs=[vmem, any_space, any_space, vmem],
-        out_specs=(any_space, vmem, vmem, vmem),
+        in_specs=[any_space, any_space, any_space, any_space, vmem],
+        out_specs=(any_space, vmem, vmem, vmem, vmem),
         scratch_shapes=scratch,
         compiler_params=pltpu.CompilerParams(
-            collective_id=0, has_side_effects=True, vmem_limit_bytes=40 * 2**20),
-    )(attn_out, grad_out, error_buf, q_start)
-
-
-def final_kernel(a_ref, pp_ref, qown_ref, g_ref, w_ref, e_ref, qq_ref,
-                 err_ref, q_ref, da_ref, lhs, acc):
-    j = pl.program_id(0)
-    tokens = a_ref.shape[0]
-
-    @pl.when(j == 0)
+            collective_id=0, has_side_effects=True, vmem_limit_bytes=56 * 2**20),
+    )(attn_out, grad_out, error_buf, proj_weight, q_start)
+
+
+def final_kernel(lhs_ref, qown_ref, d_ref, g_ref, e_ref, qq_ref, err_ref, q_ref, da_ref):
+    tokens = g_ref.shape[0]
+
+    @pl.when(pl.program_id(0) == 0)
     def _():
-        lhs[:, :tokens] = jnp.transpose(a_ref[...])
-        lhs[:, tokens:] = jnp.transpose(pp_ref[...])
         q_ref[...] = qown_ref[...]
-        acc[...] = jnp.zeros_like(acc)
-
-    g = g_ref[...]
-    moment = dot(lhs[:, :tokens], g, NN) + e_ref[0].astype(F32)
-    err_ref[0] = (moment + dot(lhs[:, tokens:], qq_ref[...], NN)).astype(BF16)
-    acc[...] += dot(g, w_ref[...], NT)
-
-    @pl.when(j == pl.num_programs(0) - 1)
-    def _():
-        da_ref[...] = acc[...].astype(BF16)
-
-
-def final(attn_out, pp, qown, g_all, proj_weight, error_buf, qq):
-    tokens, f = attn_out.shape
-    width = g_all.shape[1]
-    rank = qown.shape[0]
+        da_ref[...] = d_ref[...]
+
+    moment = dot(lhs_ref[:, :tokens], g_ref[...], NN) + e_ref[0].astype(F32)
+    err_ref[0] = (moment + dot(lhs_ref[:, tokens:], qq_ref[...], NN)).astype(BF16)
+
+
+def final(lhs, qown, d_attn, g_all, error_buf, qq):
+    tokens, width = g_all.shape
+    rank, f = qown.shape
     n = 1024
     whole = lambda shape: pl.BlockSpec(shape, lambda j: (0,) * len(shape))
     cols = lambda rows: pl.BlockSpec((rows, n), lambda j: (0, j))
@@ -393,17 +416,17 @@
             jax.ShapeDtypeStruct((rank, f), F32),
             jax.ShapeDtypeStruct((tokens, f), BF16),
         ),
-        in_specs=[whole((tokens, f)), whole((2 * rank, f)), whole((rank, f)),
-                  cols(tokens), cols(f), cols3, cols(2 * rank)],
+        in_specs=[whole((f, tokens + 2 * rank)), whole((rank, f)), whole((tokens, f)),
+                  cols(tokens), cols3, cols(2 * rank)],
         out_specs=(cols3, whole((rank, f)), whole((tokens, f))),
-        scratch_shapes=[pltpu.VMEM((f, tokens + 2 * rank), BF16), pltpu.VMEM((tokens, f), F32)],
-        compiler_params=pltpu.CompilerParams(vmem_limit_bytes=40 * 2**20),
-    )(attn_out, pp, qown, g_all, proj_weight, error_buf, qq)
+        compiler_params=pltpu.CompilerParams(vmem_limit_bytes=56 * 2**20),
+    )(lhs, qown, d_attn, g_all, error_buf, qq)
 
 
 def on_device(n_dp, n_mp, attn_out, grad_out, proj_weight, error_buf, q_start):
-    g_all, pp, qq, qown = chain(n_dp, n_mp, attn_out, grad_out, error_buf, q_start.T)
-    err, q_t, d_attn = final(attn_out, pp, qown, g_all, proj_weight, error_buf, qq)
+    g_all, lhs, qq, qown, d_attn = chain(
+        n_dp, n_mp, attn_out, grad_out, error_buf, proj_weight, q_start.T)
+    err, q_t, d_attn = final(lhs, qown, d_attn, g_all, error_buf, qq)
     return err, q_t.T, d_attn
 
 

time: 97.9 us -> 102 us (1.042)
  Pallas kernels: 93.8 us -> 101 us
  local copies, waits for them, and re-layouts: 2.91 us -> 0 us
    pallas_call x1, Pallas kernels: 77 us -> 86 us  [chain(): pl.pallas_call(functools.partial(chain_kernel, n_dp, n_mp, t), out_shape=...]
    unnamed x6 -> x0, local copies, waits for them, and re-layouts: 2.91 us -> none
    pallas_call x1, Pallas kernels: 16.8 us -> 14.6 us  [final(): pl.pallas_call(final_kernel, grid=(width // n,), out_shape=(jax.ShapeDtyp...]
where the time goes in v3:
time: 102 us; the launch traced here: 101 us
  Pallas kernels  101 us (99%)
    pallas_call x1, Pallas kernels, chain(): pl.pallas_call(functools.partial(chain_kernel, n_dp, n_mp, t), out_shape=...  86 us
    pallas_call x1, Pallas kernels, final(): pl.pallas_call(final_kernel, grid=(width // n,), out_shape=(jax.ShapeDtyp...  14.6 us

profile of v3, /device:TPU:0, one launch (start us, length us, event | category | flops | bytes accessed | tf_op | source)
XLA Modules:
  0.0 101.2 jit_solution(6040895409587854442)
XLA Ops:
  0.6 86.0 %shard_map.76 = (bf16[512,8192]{1,0:T(8,128)(2,1)}, bf16[512,576]{1,0:T(8,128)(2,1)}, bf16[64,8192]{1,0:T(8,128)(2,1)}, f32[32,512]{1,0:T(8,128)}, bf16[512,512]{1,0:T(8,128)(2,1)}) custom-call(bf16[512,512]{1,0:T(8,128)(2,1)} %a_hbm.1, bf16[32,8192]{1,0:T(8,128)(2,1)} %g_hbm.1, bf16[1,512,8192]{2,1,0:T(8,128)(2,1)} %e_ref.1, bf16[512,8192]{1,0:T(8,128)(2,1)} %w_hbm.1, ...), custom_call_target="tpu_custom_call" | custom-call | tf_op jit(solution)/shard_map/pallas_call | solution.py:375
  86.6 14.6 %shard_map.77 = (bf16[1,512,8192]{2,1,0:T(8,128)(2,1)}, f32[32,512]{1,0:T(8,128)}, bf16[512,512]{1,0:T(8,128)(2,1)}) custom-call(bf16[512,576]{1,0:T(8,128)(2,1)} %get-tuple-element.11.lhs_ref, f32[32,512]{1,0:T(8,128)} %get-tuple-element.12.qown_ref, bf16[512,512]{1,0:T(8,128)(2,1)} %get-tuple-element.13.d_ref, bf16[512,8192]{1,0:T(8,128)(2,1)} %get-tuple-element.14.g_ref, ...), custom_call_target="tpu_custom_call" | custom-call | tf_op jit(solution)/shard_map/pallas_call | solution.py:411

commit v4 on v2

--- a/solution.py
+++ b/solution.py
@@ -40,9 +40,9 @@
 
 
 def chain_kernel(n_dp, n_mp, t,
-                 a_ref, g_hbm, e_hbm, q_ref,
-                 gout, pp_ref, qq_ref, qown_ref,
-                 e_ref, g_ref, qb, gqb, pb, sx, rx, qacc, qdp, q2b, s1, u1, s2, u2,
+                 a_hbm, g_hbm, e_hbm, q_ref,
+                 gout, lhs_ref, qown_ref,
+                 a_ref, e_ref, qq_ref, g_ref, qb, gqb, pb, sx, rx, qacc, qdp, q2b, s1, u1, s2, u2,
                  send, recv, gsend, grecv, local):
     nx = n_mp // (NC * NZ)
     half = nx * NZ
@@ -69,8 +69,10 @@
     g_copy = pltpu.make_async_copy(g_hbm, g_ref, local.at[1])
     own_rows = pl.ds(pl.multiple_of(m * t, t), t)
     o_copy = pltpu.make_async_copy(g_hbm, gout.at[own_rows, :], local.at[2])
+    a_copy = pltpu.make_async_copy(a_hbm, a_ref, local.at[3])
     g_copy.start()
     e_copy.start()
+    a_copy.start()
     o_copy.start()
 
     barrier = pltpu.get_barrier_semaphore()
@@ -211,6 +213,7 @@
     wait(copies)
     gq_all = jnp.concatenate([unpack(gqb[i]) for i in range(n_mp)], axis=0)
     hi, lo = split(gq_all)
+    a_copy.wait()
     a = a_ref[...]
     pt += dot(hi, a, TN) + dot(lo, a, TN)
     pb[d] = pt
@@ -231,6 +234,7 @@
     copies = [push(sx.at[p], rx.at[m], (d, p)) for p in all_peers()]
     hop(2)
     across(1)
+    lhs_ref[:, :a_ref.shape[0]] = jnp.transpose(a_ref[...])
     wait(copies)
     total = rx[0]
     for i in range(1, n_mp):
@@ -240,8 +244,6 @@
     inv = inverse_of_factor(gram)
     pot = dot(inv, pt, NN, HP)
     o_hi, o_lo = split(-pot)
-    pp_ref[:rank, :] = o_hi
-    pp_ref[rank:, :] = o_lo
     so_hi, so_lo = split(dot(inv, s_own, NT, HP))
     stack = jnp.concatenate([o_hi, o_lo], axis=0)
     s_stack = jnp.concatenate([so_hi, so_lo], axis=0)
@@ -270,11 +272,13 @@
     q_sum = qacc[at] + u1[at].astype(F32)
     hop(3)
     across(2)
+    across(3)
     wait(copies)
     for k in range(len(chips)):
         q_sum += u2[k].astype(F32)
     qdp[d] = q_sum
-    wait([push(qdp.at[d], qdp.at[d], (p, m)) for p in d_peers])
+    copies = [push(qdp.at[d], qdp.at[d], (p, m)) for p in d_peers]
+    wait(copies)
     q_own = qdp[0]
     for k in range(1, n_dp):
         q_own += qdp[k]
@@ -283,11 +287,15 @@
 
     q2b[own] = q_own.astype(BF16)
     copies, core = gather_start(q2b)
-    across(3)
+    lhs_ref[:, a_ref.shape[0]:] = jnp.transpose(stack)
     gather_end(q2b, copies, core)
     for i, s in enumerate(slots):
         qq_ref[:rank, i * f:(i + 1) * f] = q2b[s]
         qq_ref[rank:, i * f:(i + 1) * f] = q2b[s]
+
+    q_rows = pltpu.make_async_copy(
+        qq_ref, gout.at[pl.ds(a_ref.shape[0], 2 * rank), :], local.at[4])
+    q_rows.start()
 
     for zz in range(NZ):
         for xx in range(nx):
@@ -305,6 +313,7 @@
         for xx in range(nx):
             bulk(zz, xx, c, k_core, dev(cc=1 - c)).wait_send()
     o_copy.wait()
+    q_rows.wait()
 
 
 def chain(n_dp, n_mp, attn_out, grad_out, error_buf, q_start):
@@ -319,7 +328,9 @@
     vmem = pl.BlockSpec(memory_space=pltpu.VMEM)
     block = (rank, f)
     scratch = [
+        pltpu.VMEM((tokens, f), BF16),
         pltpu.VMEM((f, width), BF16),
+        pltpu.VMEM((2 * rank, width), BF16),
         pltpu.VMEM((t, width), BF16),
         pltpu.VMEM((n_mp,) + block, BF16),
         pltpu.VMEM((n_mp, nt, 128), F32),
@@ -337,50 +348,43 @@
         pltpu.SemaphoreType.DMA((count,)),
         pltpu.SemaphoreType.DMA((2 + nx, n_mp)),
         pltpu.SemaphoreType.DMA((n_mp,)),
-        pltpu.SemaphoreType.DMA((3,)),
+        pltpu.SemaphoreType.DMA((5,)),
     ]
     return pl.pallas_call(
         functools.partial(chain_kernel, n_dp, n_mp, t),
         out_shape=(
-            jax.ShapeDtypeStruct((tokens, width), BF16),
-            jax.ShapeDtypeStruct((2 * rank, f), BF16),
-            jax.ShapeDtypeStruct((2 * rank, width), BF16),
+            jax.ShapeDtypeStruct((tokens + 2 * rank, width), BF16),
+            jax.ShapeDtypeStruct((f, tokens + 2 * rank), BF16),
             jax.ShapeDtypeStruct((rank, f), F32),
         ),
-        in_specs=[vmem, any_space, any_space, vmem],
-        out_specs=(any_space, vmem, vmem, vmem),
+        in_specs=[any_space, any_space, any_space, vmem],
+        out_specs=(any_space, vmem, vmem),
         scratch_shapes=scratch,
         compiler_params=pltpu.CompilerParams(
-            collective_id=0, has_side_effects=True, vmem_limit_bytes=40 * 2**20),
+            collective_id=0, has_side_effects=True, vmem_limit_bytes=56 * 2**20),
     )(attn_out, grad_out, error_buf, q_start)
 
 
-def final_kernel(a_ref, pp_ref, qown_ref, g_ref, w_ref, e_ref, qq_ref,
-                 err_ref, q_ref, da_ref, lhs, acc):
+def final_kernel(lhs_ref, qown_ref, g_ref, w_ref, e_ref, err_ref, q_ref, da_ref, acc):
     j = pl.program_id(0)
-    tokens = a_ref.shape[0]
+    tokens = acc.shape[0]
 
     @pl.when(j == 0)
     def _():
-        lhs[:, :tokens] = jnp.transpose(a_ref[...])
-        lhs[:, tokens:] = jnp.transpose(pp_ref[...])
         q_ref[...] = qown_ref[...]
         acc[...] = jnp.zeros_like(acc)
 
-    g = g_ref[...]
-    moment = dot(lhs[:, :tokens], g, NN) + e_ref[0].astype(F32)
-    err_ref[0] = (moment + dot(lhs[:, tokens:], qq_ref[...], NN)).astype(BF16)
-    acc[...] += dot(g, w_ref[...], NT)
+    err_ref[0] = (dot(lhs_ref[...], g_ref[...], NN) + e_ref[0].astype(F32)).astype(BF16)
+    acc[...] += dot(g_ref[:tokens, :], w_ref[...], NT)
 
     @pl.when(j == pl.num_programs(0) - 1)
     def _():
         da_ref[...] = acc[...].astype(BF16)
 
 
-def final(attn_out, pp, qown, g_all, proj_weight, error_buf, qq):
-    tokens, f = attn_out.shape
-    width = g_all.shape[1]
-    rank = qown.shape[0]
+def final(tokens, lhs, qown, g_all, proj_weight, error_buf):
+    depth, width = g_all.shape
+    rank, f = qown.shape
     n = 1024
     whole = lambda shape: pl.BlockSpec(shape, lambda j: (0,) * len(shape))
     cols = lambda rows: pl.BlockSpec((rows, n), lambda j: (0, j))
@@ -393,17 +397,16 @@
             jax.ShapeDtypeStruct((rank, f), F32),
             jax.ShapeDtypeStruct((tokens, f), BF16),
         ),
-        in_specs=[whole((tokens, f)), whole((2 * rank, f)), whole((rank, f)),
-                  cols(tokens), cols(f), cols3, cols(2 * rank)],
+        in_specs=[whole((f, depth)), whole((rank, f)), cols(depth), cols(f), cols3],
         out_specs=(cols3, whole((rank, f)), whole((tokens, f))),
-        scratch_shapes=[pltpu.VMEM((f, tokens + 2 * rank), BF16), pltpu.VMEM((tokens, f), F32)],
-        compiler_params=pltpu.CompilerParams(vmem_limit_bytes=40 * 2**20),
-    )(attn_out, pp, qown, g_all, proj_weight, error_buf, qq)
+        scratch_shapes=[pltpu.VMEM((tokens, f), F32)],
+        compiler_params=pltpu.CompilerParams(vmem_limit_bytes=56 * 2**20),
+    )(lhs, qown, g_all, proj_weight, error_buf)
 
 
 def on_device(n_dp, n_mp, attn_out, grad_out, proj_weight, error_buf, q_start):
-    g_all, pp, qq, qown = chain(n_dp, n_mp, attn_out, grad_out, error_buf, q_start.T)
-    err, q_t, d_attn = final(attn_out, pp, qown, g_all, proj_weight, error_buf, qq)
+    g_all, lhs, qown = chain(n_dp, n_mp, attn_out, grad_out, error_buf, q_start.T)
+    err, q_t, d_attn = final(attn_out.shape[0], lhs, qown, g_all, proj_weight, error_buf)
     return err, q_t.T, d_attn
 
 

time: 97.9 us -> 99.6 us (1.017)
  Pallas kernels: 93.8 us -> 98.8 us
  local copies, waits for them, and re-layouts: 2.91 us -> 0 us
    pallas_call x1, Pallas kernels: 77 us -> 80 us  [chain(): pl.pallas_call(functools.partial(chain_kernel, n_dp, n_mp, t), out_shape=...]
    unnamed x6 -> x0, local copies, waits for them, and re-layouts: 2.91 us -> none
    pallas_call x1, Pallas kernels: 16.8 us -> 18.7 us  [final(): pl.pallas_call(final_kernel, grid=(width // n,), out_shape=(jax.ShapeDtyp...]
where the time goes in v4:
time: 99.6 us; the launch traced here: 99.4 us
  Pallas kernels  98.8 us (99%)
    pallas_call x1, Pallas kernels, chain(): pl.pallas_call(functools.partial(chain_kernel, n_dp, n_mp, t), out_shape=...  80 us
    pallas_call x1, Pallas kernels, final(): pl.pallas_call(final_kernel, grid=(width // n,), out_shape=(jax.ShapeDtyp...  18.7 us

profile of v4, /device:TPU:0, one launch (start us, length us, event | category | flops | bytes accessed | tf_op | source)
XLA Modules:
  0.0 99.4 jit_solution(8718478011008021117)
XLA Ops:
  0.6 80.0 %shard_map.76 = (bf16[576,8192]{1,0:T(8,128)(2,1)}, bf16[512,576]{1,0:T(8,128)(2,1)}, f32[32,512]{1,0:T(8,128)}) custom-call(bf16[512,512]{1,0:T(8,128)(2,1)} %a_hbm.1, bf16[32,8192]{1,0:T(8,128)(2,1)} %g_hbm.1, bf16[1,512,8192]{2,1,0:T(8,128)(2,1)} %e_ref.1, f32[32,512]{1,0:T(8,128)} %bitcast.2), custom_call_target="tpu_custom_call" | custom-call | tf_op jit(solution)/shard_map/pallas_call | solution.py:353
  80.7 18.7 %shard_map.77 = (bf16[1,512,8192]{2,1,0:T(8,128)(2,1)}, f32[32,512]{1,0:T(8,128)}, bf16[512,512]{1,0:T(8,128)(2,1)}) custom-call(bf16[512,576]{1,0:T(8,128)(2,1)} %get-tuple-element.9.lhs_ref, f32[32,512]{1,0:T(8,128)} %get-tuple-element.10.qown_ref, bf16[576,8192]{1,0:T(8,128)(2,1)} %get-tuple-element.11.g_ref, bf16[512,8192]{1,0:T(8,128)(2,1)} %w_ref.1, ...), custom_call_target="tpu_custom_call" | custom-call | tf_op jit(solution)/shard_map/pallas_call | solution.py:392
